TPU v7x, 256 devices: a whole 4x4x8 slice. The times are simulated.
256 devices in a mesh: seq: 32 (over z, y), head: 8 (over x, core).
Axes of the slice: x: 4, y: 4, z: 8, core: 2. Of those that a mesh axis runs over, the one named last changes fastest.
Arguments:
- grad_y: bfloat16 [16384, 4096], P('seq', 'head'), may hold values from -6 to 6
- w_out: bfloat16 [4096, 4096], P('head'), may hold values from -0.09375 to 0.09375
- queries: bfloat16 [16384, 4096], P('seq', 'head'), may hold values from -6 to 6
- keys: bfloat16 [16384, 4096], P('seq', 'head'), may hold values from -6 to 6
- values: bfloat16 [16384, 4096], P('seq', 'head'), may hold values from -6 to 6
- level_rows: int32 [16384], P('seq'), may hold values from 0 to 127
- level_table: float32 [128, 12, 32], P(None, None, 'head'), may hold values from 0.2 to 3
Outputs:
- query_grad: float32 [16384, 4096], P('seq', 'head')
- key_grad: float32 [16384, 4096], P('seq', 'head')
- value_grad: float32 [16384, 4096], P('seq', 'head')
Inputs may be any that keep to these rules, and one draw needn't show every extreme that they name: `level_rows`: each token names one row of the level-weight table.
All inputs are finite; a program needn't handle non-finite values.
Results may differ from a plain program's by a relative error of at most 0.0049.
Values may be sent and summed in bfloat16 or wider, within the bound.
A program may use at most 128 MiB of HBM per device.

v0:
```python
import jax
import jax.numpy as jnp
from jax import lax
from jax.sharding import PartitionSpec as P

BLK = 128


def level_norm(level_count, block_size, head_size):
    level_ids = jnp.arange(level_count, dtype=jnp.int32)
    doubling = jnp.exp2(jnp.maximum(level_ids - 1, 0).astype(jnp.float32))
    return lax.rsqrt(doubling * float(block_size * head_size))


def sibling(states, bit_index):
    block_count = states.shape[0]
    span = 2**bit_index
    grouped = states.reshape((block_count // span, span) + states.shape[1:]).sum(axis=1)
    paired = grouped.reshape((block_count // (2 * span), 2) + grouped.shape[1:])[:, ::-1]
    return jnp.repeat(paired.reshape(grouped.shape), span, axis=0)


def shards(grad_y, w_out, queries, keys, values, level_rows, level_table):
    token_count, width = queries.shape
    table_size, level_count, head_count = level_table.shape
    head_size = width // head_count
    block_count = token_count // BLK
    local_bits = block_count.bit_length() - 1
    device_bits = lax.axis_size("seq").bit_length() - 1
    position = lax.axis_index("seq")
    highest = lax.Precision.HIGHEST
    columns = w_out
    grad_sum = lax.dot_general(
        lax.all_gather(grad_y, "head", axis=1, tiled=True),
        columns,
        (((1,), (1,)), ((), ())),
        preferred_element_type=jnp.float32,
    )
    grad_out = grad_sum.astype(jnp.bfloat16)
    one_hot = (level_rows[:, None] == jnp.arange(table_size, dtype=jnp.int32)[None, :]).astype(
        jnp.float32
    )
    weights = jnp.dot(
        one_hot, level_table.reshape(table_size, level_count * head_count), precision=highest
    )
    weights = (
        weights.reshape(token_count, level_count, head_count)
        * level_norm(level_count, BLK, head_size)[None, :, None]
    )
    block_shape = (block_count, BLK, head_count, head_size)
    query_blocks = queries.reshape(block_shape)
    key_blocks = keys.reshape(block_shape)
    value_blocks = values.reshape(block_shape)
    grad_blocks = grad_out.reshape(block_shape)
    weight_blocks = weights.reshape(block_count, BLK, level_count, head_count)
    causal = (jnp.arange(BLK)[:, None] >= jnp.arange(BLK)[None, :]).astype(jnp.float32)
    intra_weight = jnp.transpose(weight_blocks[:, :, 0, :], (0, 2, 1))[:, :, :, None] * causal
    intra_grad = (
        jnp.einsum("bthp,bshp->bhts", grad_blocks, value_blocks, preferred_element_type=jnp.float32)
        * intra_weight
    ).astype(jnp.bfloat16)
    intra_score = (
        jnp.einsum("bthp,bshp->bhts", query_blocks, key_blocks, preferred_element_type=jnp.float32)
        * intra_weight
    ).astype(jnp.bfloat16)
    query_grad = jnp.einsum(
        "bhts,bshp->bthp", intra_grad, key_blocks, preferred_element_type=jnp.float32
    )
    key_grad = jnp.einsum(
        "bhts,bthp->bshp", intra_grad, query_blocks, preferred_element_type=jnp.float32
    )
    value_grad = jnp.einsum(
        "bhts,bthp->bshp", intra_score, grad_blocks, preferred_element_type=jnp.float32
    )
    states = jnp.einsum(
        "bthi,bthj->bhij", key_blocks, value_blocks, preferred_element_type=jnp.float32
    )
    block_ids = jnp.arange(block_count, dtype=jnp.int32)
    adjoint = jnp.zeros_like(states)
    for bit_index in range(local_bits):
        present = (block_ids >> bit_index & 1).astype(jnp.float32)[:, None, None, None]
        bucket = (sibling(states, bit_index) * present).astype(jnp.bfloat16)
        level_weight = weight_blocks[:, :, bit_index + 1, :][..., None]
        query_grad = query_grad + level_weight * jnp.einsum(
            "bthj,bhij->bthi", grad_blocks, bucket, preferred_element_type=jnp.float32
        )
        weighted = (level_weight * query_blocks).astype(jnp.bfloat16)
        adjoint_part = (
            jnp.einsum("bthi,bthj->bhij", weighted, grad_blocks, preferred_element_type=jnp.float32)
            * present
        )
        adjoint = adjoint + sibling(adjoint_part, bit_index)
    flat_query = queries.reshape(token_count, head_count, head_size)
    flat_grad = grad_out.reshape(token_count, head_count, head_size)
    device_total = states.sum(axis=0)
    device_flags = [
        (position >> bit_index & 1).astype(jnp.float32) for bit_index in range(device_bits)
    ]
    device_parts = []
    for bit_index in range(device_bits):
        level_weight = weights[:, local_bits + bit_index + 1, :][..., None]
        weighted = (level_weight * flat_query).astype(jnp.bfloat16)
        device_parts.append(
            jnp.einsum("thi,thj->hij", weighted, flat_grad, preferred_element_type=jnp.float32)
            * device_flags[bit_index]
        )

    def membership(row_count):
        peers = jnp.arange(row_count, dtype=jnp.int32)
        columns = []
        for bit_index in range(device_bits):
            inside = (
                (peers >> bit_index + 1 == position >> bit_index + 1)
                & (peers >> bit_index & 1 == 0)
                & (position >> bit_index & 1 == 1)
            )
            columns.append(inside.astype(jnp.float32))
        return jnp.stack(columns, axis=1)

    segment = lax.all_gather(device_total[None], "seq", axis=0, tiled=True)
    stacked = jnp.einsum("ne,nhij->ehij", membership(segment.shape[0]), segment, precision=highest)
    buckets = [stacked[bit_index] for bit_index in range(device_bits)]
    adjoint_stack = jnp.stack(device_parts, axis=0)
    carried = lax.psum_scatter(
        jnp.einsum(
            "ne,ehij->nhij", membership(lax.axis_size("seq") * 1), adjoint_stack, precision=highest
        ),
        "seq",
        scatter_dimension=0,
        tiled=True,
    )[0]
    for bit_index in range(device_bits):
        level_weight = weight_blocks[:, :, local_bits + bit_index + 1, :][..., None]
        query_grad = query_grad + level_weight * jnp.einsum(
            "bthj,hij->bthi",
            grad_blocks,
            buckets[bit_index].astype(jnp.bfloat16),
            preferred_element_type=jnp.float32,
        )
    adjoint_all = (adjoint + carried[None]).astype(jnp.bfloat16)
    key_grad = key_grad + jnp.einsum(
        "bshj,bhij->bshi", value_blocks, adjoint_all, preferred_element_type=jnp.float32
    )
    value_grad = value_grad + jnp.einsum(
        "bshi,bhij->bshj", key_blocks, adjoint_all, preferred_element_type=jnp.float32
    )
    return (
        query_grad.reshape(token_count, width),
        key_grad.reshape(token_count, width),
        value_grad.reshape(token_count, width),
    )


def solution(mesh):
    return jax.shard_map(
        shards,
        mesh=mesh,
        in_specs=(
            P("seq", "head"),
            P("head", None),
            P("seq", "head"),
            P("seq", "head"),
            P("seq", "head"),
            P("seq"),
            P(None, None, "head"),
        ),
        out_specs=(P("seq", "head"), P("seq", "head"), P("seq", "head")),
        check_vma=False,
    )
```

profile of v0, /device:TPU:1, one launch (start us, length us, event | category | flops | bytes accessed | tf_op | source)
XLA Modules:
  0.0 387.6 jit_solution(12083027111815541625)
XLA Ops:
  7.2 0.7 all-gather.4.cloned.1.call-update
  8.0 1.2 reshape.258
  9.1 1.4 reshape.261
  10.5 1.1 bitcast_reduce_fusion.1
  11.7 0.8 reduce_sum.28
  13.0 1.3 copy.198
  14.4 34.4 %all-gather.4.cloned.1.call-done = bf16[512,4096]{1,0:T(8,128)(2,1)} async-done(((bf16[512,512]{1,0:T(8,128)(2,1)}), bf16[512,4096]{1,0:T(8,128)(2,1)}) %all-gather.4.cloned.1.call-update) | async-done | bytes 4194320 | tf_op jit(solution)/shard_map/all_gather | solution.py:34
  48.7 5.8 %convolution_convert_fusion = bf16[512,512]{0,1:T(8,128)(2,1)S(1)} fusion(bf16[512,4096]{1,0:T(8,128)(2,1)} %all-gather.4.cloned.1.call-done, bf16[512,4096]{1,0:T(8,128)(2,1)} %param.8), kind=kOutput, calls=%fused_computation.40 | convolution fusion | flops 2147745792 | bytes 8912896 | tf_op jit(solution)/shard_map/dot_general | solution.py:33
  56.2 3.9 %fusion.2 = f32[32,4,128,128]{3,0,2,1:T(8,128)S(1)} fusion(f32[5,4,128,128]{3,2,1,0:T(8,128)S(1)} %fusion.27, pred[32,5]{0,1:T(8,128)(4,1)S(1)} %stack.17), kind=kOutput, calls=%fused_computation.2 | convolution fusion | flops 125829120 | bytes 9699488 | tf_op jit(solution)/shard_map/ne,ehij->nhij/dot_general | solution.py:125
  60.1 8.3 %copy.168 = f32[32,4,128,128]{3,2,1,0:T(8,128)} copy(f32[32,4,128,128]{3,0,2,1:T(8,128)S(1)} %fusion.2) | data formatting | bytes 16777216 | tf_op jit(solution)/shard_map/ne,ehij->nhij/dot_general | solution.py:125
  68.4 1.0 copy-done.8
  69.6 1.1 rev.8
  70.7 0.8 reverse.6
  71.6 2.0 fusion.39
  73.9 0.8 bitcast_reduce_fusion
  74.8 1.0 convolution_multiply_fusion.1
  75.8 1.1 reverse_add_fusion
  76.9 2.6 copy.156
  80.0 1.3 convolution_bitcast_fusion.1
  81.3 1.3 convolution_bitcast_fusion.9
  82.6 1.7 fusion.25
  84.3 1.9 fusion.22
  86.2 1.6 fusion.20
  87.7 61.4 %all-gather.6.cloned.1.call-done = f32[128,128,128]{2,1,0:T(8,128)} async-done(((f32[4,128,128]{2,1,0:T(8,128)}), f32[128,128,128]{2,1,0:T(8,128)}) %all-gather.6.cloned.1.call-update) | async-done | bytes 8388624 | tf_op jit(solution)/shard_map/all_gather | solution.py:120
  149.1 10.5 %fusion.4 = bf16[5,4,128,128]{3,0,2,1:T(8,128)(2,1)S(1)} fusion(f32[32,4,128,128]{3,2,1,0:T(8,128)} %bitcast.212, pred[32,5]{0,1:T(8,128)(4,1)S(1)} %stack.17), kind=kOutput, calls=%fused_computation.6 | convolution fusion | flops 126156800 | bytes 9044128 | tf_op jit(solution)/shard_map/ne,nhij->ehij/dot_general | solution.py:121
  159.6 1.0 fusion.96
  164.1 0.7 copy.148
  164.8 1.0 copy.312
  165.8 210.0 %reduce-scatter.2.cloned.1.call-done = f32[1,4,128,128]{3,2,1,0:T(8,128)} async-done(((f32[32,4,128,128]{3,2,1,0:T(8,128)}), f32[1,4,128,128]{3,2,1,0:T(8,128)}) %reduce-scatter.2.cloned.1.call-update) | async-done | bytes 262160 | tf_op jit(solution)/shard_map/reduce_scatter | solution.py:124
  375.8 1.1 copy.169
  378.1 1.0 copy.311
  380.0 1.0 copy.310
  (73 shorter events, 8.9 us)
Async XLA Ops:
  7.2 5.4 %copy-start = (f32[128,12,4]{0,2,1:T(4,128)S(1)}, f32[128,12,4]{0,2,1:T(4,128)}, u32[]{:S(2)}) copy-start(f32[128,12,4]{0,2,1:T(4,128)} %param.13) | copy-start | bytes 73732
  7.2 41.6 %all-gather.4.cloned.1.call-start = ((), (), s32[]{:S(2)}) async-start(), calls=%async_computation.1 | async-start | bytes 4718592 | tf_op jit(solution)/shard_map/all_gather | solution.py:34
  7.9 141.2 %all-gather.6.cloned.1.call-start = ((), (), s32[]{:S(2)}) async-start(), calls=%async_computation.3 | async-start | bytes 8650752 | tf_op jit(solution)/shard_map/all_gather | solution.py:120
  9.1 3.3 copy-start.2
  10.5 2.1 copy-start.12
  12.5 363.3 %reduce-scatter.2.cloned.1.call-start = ((), (), s32[]{:S(2)}) async-start(), calls=%async_computation.2 | async-start | bytes 8650752 | tf_op jit(solution)/shard_map/reduce_scatter | solution.py:124
  68.4 1.0 copy-start.8
  69.5 1.1 copy-start.9
  70.7 2.9 copy-start.7
  75.8 3.6 copy-start.3
  84.3 1.9 copy-start.10
  159.6 1.2 copy-start.5
  164.1 212.8 %copy-start.6 = (f32[2,2,4,128,128]{3,4,2,1,0:T(8,128)S(1)}, f32[2,2,4,128,128]{3,4,2,1,0:T(8,128)}, u32[]{:S(2)}) copy-start(f32[2,2,4,128,128]{3,4,2,1,0:T(8,128)} %copy.156) | copy-start | bytes 3145732
  164.8 212.3 %copy-start.4 = (f32[4,128,4,128]{3,1,2,0:T(8,128)S(1)}, f32[4,128,4,128]{3,1,2,0:T(8,128)}, u32[]{:S(2)}) copy-start(f32[4,128,4,128]{3,1,2,0:T(8,128)} %convolution_bitcast_fusion.1) | copy-start | bytes 3145732
  377.4 1.7 copy-start.11
  379.1 1.9 copy-start.1
Sparse Core Ops, SparseCore 0:
  9.9 38.8 all-gather.3
  51.3 97.7 all-gather.5
  153.1 222.6 reduce-scatter.1
where the time goes:
time: 391 us; the launch traced here: 388 us
  waiting for transfers between devices  306 us (78%)
  matrix products  37.4 us (10%)
  local copies, waits for them, and re-layouts  25.1 us (6%)
  between operations  14.2 us (4%)
  other arithmetic  4.27 us (1%)
    reduce_scatter x1, waiting for transfers between devices, shards(): lax.psum_scatter(jnp.einsum('ne,ehij->nhij', membership(lax.axis_size('se...  210 us
    all_gather x1, waiting for transfers between devices, shards(): segment = lax.all_gather(device_total[None], 'seq', axis=0, tiled=True)  61.4 us
    all_gather x1, waiting for transfers between devices, shards(): lax.all_gather(grad_y, 'head', axis=1, tiled=True)  34.4 us
    dot_general x1, matrix products, shards(): jnp.einsum('ne,nhij->ehij', membership(segment.shape[0]), segment, precis...  10.5 us
    dot_general x1, local copies, waits for them, and re-layouts, shards(): jnp.einsum('ne,ehij->nhij', membership(lax.axis_size('seq') * 1), adjoint...  8.28 us
  transfers between devices with their start and end apart: 3, of which 3 were waited for; matrix products, arithmetic and copies ran while one was open for 16% of the time, Pallas kernels for 0%

commit v1 on v0

v1 whole, which is shorter than its diff:
```python
import functools

import jax
import jax.numpy as jnp
from jax import lax
from jax.experimental import pallas as pl
from jax.experimental.pallas import tpu as pltpu
from jax.sharding import PartitionSpec as P

BLK = 128
CORES = 2
MESH = pl.DeviceIdType.MESH
NN = (((1,), (0,)), ((), ()))
NT = (((1,), (1,)), ((), ()))
TN = (((0,), (0,)), ((), ()))
F32 = jnp.float32
BF16 = jnp.bfloat16


def dot(a, b, dims=NN):
    return lax.dot_general(a, b, dims, preferred_element_type=F32)


def layer(
    seq_size, head_size, heads,
    y, w, q, k, v, rows, table,
    qg_out, kg_out, vg_out,
    yb, wb, qb, kb, vb, gb, qg, kg, vg,
    wrow, wcol, wq, score, state, local_bucket, local_adjoint,
    total, bucket_in, bucket_sum, bucket,
    part, part_in, part_sum, carried,
    load_sem, own_sem, send_sem, y_sem,
    bs1, br1, bs2, br2, as1, ar1, as2, ar2, out_sem,
):
    tokens, feats = y.shape
    width = heads * BLK
    blocks = tokens // BLK
    local_bits = blocks.bit_length() - 1
    device_bits = seq_size.bit_length() - 1
    levels = 1 + local_bits + device_bits
    ring = head_size // CORES
    pos = lax.axis_index("seq")
    head = lax.axis_index("head")
    x, core = head // CORES, lax.rem(head, CORES)
    right = lax.rem(x + 1, ring) * CORES + core
    left = lax.rem(x + ring - 1, ring) * CORES + core
    across = lax.rem(x + 2, ring) * CORES + core
    twin = x * CORES + 1 - core

    loads = [
        pltpu.make_async_copy(src, dst, load_sem.at[n])
        for n, (src, dst) in enumerate(((k, kb), (v, vb), (q, qb), (w, wb)))
    ]
    for load in loads:
        load.start()

    bucket[...] = jnp.zeros_like(bucket)
    carried[...] = jnp.zeros_like(carried)

    barrier = pltpu.get_barrier_semaphore()

    def greet(step, _):
        peer = lax.rem(pos + step, seq_size)
        pl.semaphore_signal(barrier, inc=1, device_id=(peer, head), device_id_type=MESH)
        return 0

    for peer in (right, left, twin):
        pl.semaphore_signal(barrier, inc=1, device_id=(pos, peer), device_id_type=MESH)
    lax.fori_loop(1, seq_size, greet, 0)
    pl.semaphore_wait(barrier, seq_size - 1 + 3)

    def columns(owner):
        return pl.ds(pl.multiple_of(owner * feats, feats), feats)

    def place(owner, row, count):
        return yb.at[pl.ds(row, count), columns(owner)]

    def send(src, dst, sem_out, sem_in, peer):
        pltpu.make_async_remote_copy(
            src_ref=src, dst_ref=dst, send_sem=sem_out, recv_sem=sem_in,
            device_id=peer, device_id_type=MESH,
        ).start()

    for b in range(blocks):
        src = y.at[pl.ds(b * BLK, BLK), :]
        for n, peer in enumerate((right, left, twin)):
            send(src, place(head, b * BLK, BLK), own_sem.at[n], y_sem.at[head, b], (pos, peer))
        pltpu.make_async_copy(src, place(head, b * BLK, BLK), y_sem.at[head, b]).start()

    def wait_y(owner, b):
        here = place(owner, b * BLK, BLK)
        pltpu.make_async_copy(here, here, y_sem.at[owner, b]).wait()

    half = BLK // 2

    def forward_near(b):
        wait_y(left, b)
        piece = place(left, b * BLK, half)
        send(piece, piece, send_sem.at[0], y_sem.at[left, b], (pos, right))
        piece = place(left, b * BLK, BLK)
        send(piece, piece, send_sem.at[2], y_sem.at[left, b], (pos, twin))
        wait_y(right, b)
        piece = place(right, b * BLK + half, half)
        send(piece, piece, send_sem.at[1], y_sem.at[right, b], (pos, left))
        piece = place(right, b * BLK, BLK)
        send(piece, piece, send_sem.at[3], y_sem.at[right, b], (pos, twin))

    def forward_far(b):
        wait_y(across, b)
        piece = place(across, b * BLK, BLK)
        send(piece, piece, send_sem.at[4], y_sem.at[across, b], (pos, twin))

    def finish_y(b):
        wait_y(head, b)
        wait_y(twin, b)
        for owner in (left, right, across):
            wait_y(owner + 1 - 2 * core, b)

    def project(b):
        at = pl.ds(b * BLK, BLK)
        gb[at, :] = dot(yb[at, :], wb[...], NT).astype(BF16)

    def spans(bit):
        count = 2 << bit
        return count, width // count, lax.rem(pos, count)

    def scatter_rows(bit, src_bit, data, landing, result, sem_out, sem_in, sem_result):
        count, size, index = spans(bit)

        @pl.when(lax.rem(pos // (1 << bit), 2) == src_bit)
        def _():
            if bit == 0:
                send(data, result.at[0], sem_out.at[0], sem_result.at[0], (pos + 1 - 2 * src_bit, head))
                return
            slot = landing.at[bit, pl.ds(pl.multiple_of(lax.rem(index, 1 << bit) * size, size), size), :]

            def step(off, _):
                owner = lax.rem(index + off, count)
                src = data.at[pl.ds(pl.multiple_of(owner * size, size), size), :]
                send(src, slot, sem_out.at[bit], sem_in.at[bit], (pos - index + owner, head))
                return 0

            lax.fori_loop(1, count, step, 0)
            src = data.at[pl.ds(pl.multiple_of(index * size, size), size), :]
            pltpu.make_async_copy(src, slot, sem_in.at[bit]).start()

    def sum_rows(bit, src_bit, landing, summed, result, sem_in, sem_out, sem_result):
        if bit == 0:
            return
        count, size, index = spans(bit)
        here = landing.at[bit]
        pltpu.make_async_copy(here, here, sem_in.at[bit]).wait()
        value = landing[bit, 0:size, :].astype(F32)
        for n in range(1, 1 << bit):
            value = value + landing[bit, n * size:(n + 1) * size, :].astype(F32)
        summed[bit, 0:size, :] = value.astype(BF16)
        src = summed.at[bit, pl.ds(0, size), :]
        dst = result.at[bit, pl.ds(pl.multiple_of(index * size, size), size), :]
        first = (1 - src_bit) * (1 << bit)
        own = lax.rem(index, 1 << bit)
        sink = lax.rem(pos // (1 << bit), 2) != src_bit

        def step(off, _):
            peer = first + lax.rem(own + off, 1 << bit)
            send(src, dst, sem_out.at[bit], sem_result.at[bit], (pos - index + peer, head))
            return 0

        lax.fori_loop(1, 1 << bit, step, 0)

        @pl.when(sink)
        def _():
            pltpu.make_async_copy(src, dst, sem_result.at[bit]).start()

        @pl.when(jnp.logical_not(sink))
        def _():
            step(0, 0)

    def wait_result(bit, src_bit, result, sem_result):
        @pl.when(lax.rem(pos // (1 << bit), 2) != src_bit)
        def _():
            here = result.at[bit]
            pltpu.make_async_copy(here, here, sem_result.at[bit]).wait()

    def drain(bit, src_bit, data, landing, sem_first, sem_second):
        count, size, _ = spans(bit)
        source = lax.rem(pos // (1 << bit), 2) == src_bit

        @pl.when(source)
        def _():
            sent = data if bit == 0 else data.at[pl.ds(0, width - size), :]
            pltpu.make_async_copy(sent, sent, sem_first.at[bit]).wait()
            if bit > 0:
                again = landing.at[bit]
                pltpu.make_async_copy(again, again, sem_second.at[bit]).wait()

        if bit > 0:
            @pl.when(jnp.logical_not(source))
            def _():
                again = landing.at[bit, pl.ds(0, width // 2 - size), :]
                pltpu.make_async_copy(again, again, sem_second.at[bit]).wait()

    loads[0].wait()
    loads[1].wait()
    lanes = [slice(h * BLK, (h + 1) * BLK) for h in range(heads)]
    for h in range(heads):
        sums = jnp.zeros((BLK, BLK), F32)
        for b in range(blocks):
            at = slice(b * BLK, (b + 1) * BLK)
            value = dot(kb[at, lanes[h]], vb[at, lanes[h]], TN)
            state[b, lanes[h], :] = value
            sums = sums + value
        total[lanes[h], :] = sums.astype(BF16)
    for bit in reversed(range(device_bits)):
        scatter_rows(bit, 0, total, bucket_in, bucket, bs1, br1, br2)

    level = lax.rem(lax.broadcasted_iota(jnp.int32, table.shape, 0), levels)
    norm = jnp.zeros(table.shape, F32)
    for n in range(levels):
        norm = jnp.where(level == n, (BLK * BLK * 2.0 ** max(n - 1, 0)) ** -0.5, norm)
    scaled = table[...] * norm
    hot = (lax.broadcasted_iota(jnp.int32, (table.shape[1], tokens), 0) == rows[...]).astype(BF16)
    weight = jnp.zeros((table.shape[0], tokens), F32)
    for _ in range(3):
        piece = scaled.astype(BF16)
        scaled = scaled - piece.astype(F32)
        weight = weight + dot(piece, hot)
    wrow[...] = weight
    padded = jnp.concatenate([weight, jnp.zeros((BLK - weight.shape[0], tokens), F32)], axis=0)
    for b in range(blocks):
        at = slice(b * BLK, (b + 1) * BLK)
        wcol[at, :] = padded[:, at].T

    for m in range(local_bits):
        for b in range(blocks):
            if b >> m & 1:
                first = ((b >> m) ^ 1) << m
                value = state[first]
                for n in range(first + 1, first + (1 << m)):
                    value = value + state[n]
                local_bucket[b, m] = value.astype(BF16)
            else:
                local_bucket[b, m] = jnp.zeros((width, BLK), BF16)

    loads[2].wait()
    row_id = lax.broadcasted_iota(jnp.int32, (BLK, BLK), 0)
    col_id = lax.broadcasted_iota(jnp.int32, (BLK, BLK), 1)
    forward_near(0)
    for h in range(heads):
        for b in range(blocks):
            at = slice(b * BLK, (b + 1) * BLK)
            value = dot(kb[at, lanes[h]], qb[at, lanes[h]], NT)
            value = value * jnp.where(col_id >= row_id, wrow[h * levels:h * levels + 1, at], 0.0)
            score[b, lanes[h], :] = value.astype(BF16)
    forward_near(1)
    for bit in reversed(range(device_bits)):
        sum_rows(bit, 0, bucket_in, bucket_sum, bucket, br1, bs2, br2)
    for h in range(heads):
        for b in range(blocks):
            at = slice(b * BLK, (b + 1) * BLK)
            turned = qb[at, lanes[h]].astype(F32).T
            for n in range(1, levels):
                value = turned * wrow[h * levels + n:h * levels + n + 1, at]
                wq[h, (n - 1) * BLK:n * BLK, at] = value.astype(BF16)
    forward_near(2)
    forward_far(0)
    loads[3].wait()
    finish_y(0)
    project(0)
    forward_near(3)
    forward_far(1)
    finish_y(1)
    project(1)
    forward_far(2)
    finish_y(2)
    project(2)
    forward_far(3)
    finish_y(3)
    project(3)

    for h in range(heads):
        for bit in range(device_bits):
            n = local_bits + bit
            value = dot(wq[h, n * BLK:(n + 1) * BLK, :], gb[:, lanes[h]])
            part[bit, lanes[h], :] = value.astype(BF16)
    for bit in reversed(range(device_bits)):
        scatter_rows(bit, 1, part.at[bit], part_in, carried, as1, ar1, ar2)

    for h in range(heads):
        sums = [jnp.zeros((BLK, BLK), F32) for _ in range(blocks)]
        for m in range(local_bits):
            for u in range(1, blocks >> m, 2):
                at = slice(u << m << 7, (u + 1) << m << 7)
                value = dot(wq[h, m * BLK:(m + 1) * BLK, at], gb[at, lanes[h]])
                for j in range((u - 1) << m, u << m):
                    sums[j] = sums[j] + value
        for j in range(blocks):
            local_adjoint[j, lanes[h], :] = sums[j]

    def inner(b, _):
        at = pl.ds(pl.multiple_of(b * BLK, BLK), BLK)
        for h in range(heads):
            grad, key = gb[at, lanes[h]], kb[at, lanes[h]]
            value = dot(grad, vb[at, lanes[h]], NT)
            value = jnp.where(row_id >= col_id, value * wcol[at, h * levels:h * levels + 1], 0.0)
            intra = value.astype(BF16)
            kg[at, lanes[h]] = dot(intra, qb[at, lanes[h]], TN)
            vg[at, lanes[h]] = dot(score[b, lanes[h], :], grad)
            value = dot(intra, key)
            for m in range(local_bits):
                n = h * levels + 1 + m
                value = value + wcol[at, n:n + 1] * dot(grad, local_bucket[b, m, lanes[h], :], NT)
            qg[at, lanes[h]] = value
        return 0

    lax.fori_loop(0, blocks, inner, 0)
    for bit in reversed(range(device_bits)):
        sum_rows(bit, 1, part_in, part_sum, carried, ar1, as2, ar2)
    for bit in range(device_bits):
        wait_result(bit, 0, bucket, br2)

    def outer(b, _):
        at = pl.ds(pl.multiple_of(b * BLK, BLK), BLK)
        for h in range(heads):
            grad = gb[at, lanes[h]]
            value = qg[at, lanes[h]]
            for bit in range(device_bits):
                n = h * levels + 1 + local_bits + bit
                value = value + wcol[at, n:n + 1] * dot(grad, bucket[bit, lanes[h], :], NT)
            qg[at, lanes[h]] = value
        return 0

    lax.fori_loop(0, blocks, outer, 0)
    out_q = pltpu.make_async_copy(qg, qg_out, out_sem.at[0])
    out_q.start()

    for bit in range(device_bits):
        wait_result(bit, 1, carried, ar2)
    for h in range(heads):
        sums = carried[0, lanes[h], :].astype(F32)
        for bit in range(1, device_bits):
            sums = sums + carried[bit, lanes[h], :].astype(F32)
        for b in range(blocks):
            at = slice(b * BLK, (b + 1) * BLK)
            adjoint = (local_adjoint[b, lanes[h], :] + sums).astype(BF16)
            kg[at, lanes[h]] += dot(vb[at, lanes[h]], adjoint, NT)
            vg[at, lanes[h]] += dot(kb[at, lanes[h]], adjoint)
    out_k = pltpu.make_async_copy(kg, kg_out, out_sem.at[1])
    out_v = pltpu.make_async_copy(vg, vg_out, out_sem.at[2])
    out_k.start()
    out_v.start()

    for bit in range(device_bits):
        drain(bit, 0, total, bucket_in, bs1, bs2)
        drain(bit, 1, part.at[bit], part_in, as1, as2)
    for n in range(3):
        pltpu.make_async_copy(y, y, own_sem.at[n]).wait()
    for n in range(5):
        sent = yb.at[pl.ds(0, tokens // 2 if n < 2 else tokens), pl.ds(0, feats)]
        pltpu.make_async_copy(sent, sent, send_sem.at[n]).wait()
    out_q.wait()
    out_k.wait()
    out_v.wait()


def shards(grad_y, w_out, queries, keys, values, level_rows, level_table):
    tokens, width = queries.shape
    feats = grad_y.shape[1]
    heads = level_table.shape[2]
    blocks = tokens // BLK
    seq_size, head_size = lax.axis_size("seq"), lax.axis_size("head")
    device_bits = seq_size.bit_length() - 1
    local_bits = blocks.bit_length() - 1
    levels = 1 + local_bits + device_bits
    table = level_table[:, :levels, :].transpose(2, 1, 0).reshape(heads * levels, level_table.shape[0])
    hbm = pl.BlockSpec(memory_space=pl.ANY)
    vmem = pl.BlockSpec(memory_space=pltpu.VMEM)
    dma = pltpu.SemaphoreType.DMA
    tree = [
        pltpu.VMEM((device_bits, width // 2, BLK), BF16),
        pltpu.VMEM((device_bits, width // 4, BLK), BF16),
        pltpu.VMEM((device_bits, width, BLK), BF16),
    ]
    out = jax.ShapeDtypeStruct((tokens, width), F32)
    return pl.pallas_call(
        functools.partial(layer, seq_size, head_size, heads),
        out_shape=(out, out, out),
        in_specs=[hbm] * 5 + [vmem] * 2,
        out_specs=(hbm,) * 3,
        scratch_shapes=[
            pltpu.VMEM((tokens, head_size * feats), BF16),
            pltpu.VMEM(w_out.shape, BF16),
            pltpu.VMEM((tokens, width), BF16),
            pltpu.VMEM((tokens, width), BF16),
            pltpu.VMEM((tokens, width), BF16),
            pltpu.VMEM((tokens, width), BF16),
            pltpu.VMEM((tokens, width), F32),
            pltpu.VMEM((tokens, width), F32),
            pltpu.VMEM((tokens, width), F32),
            pltpu.VMEM((heads * levels, tokens), F32),
            pltpu.VMEM((tokens, BLK), F32),
            pltpu.VMEM((heads, (levels - 1) * BLK, tokens), BF16),
            pltpu.VMEM((blocks, width, BLK), BF16),
            pltpu.VMEM((blocks, width, BLK), F32),
            pltpu.VMEM((blocks, local_bits, width, BLK), BF16),
            pltpu.VMEM((blocks, width, BLK), F32),
            pltpu.VMEM((width, BLK), BF16),
            *tree,
            pltpu.VMEM((device_bits, width, BLK), BF16),
            *tree,
            dma((4,)),
            dma((3,)),
            dma((5,)),
            dma((head_size, blocks)),
            *[dma((device_bits,))] * 8,
            dma((3,)),
        ],
        compiler_params=pltpu.CompilerParams(
            collective_id=0, has_side_effects=True, vmem_limit_bytes=56 * 2**20
        ),
        name="layer",
    )(grad_y, w_out, queries, keys, values, level_rows.reshape(1, tokens), table)


def solution(mesh):
    return jax.shard_map(
        shards,
        mesh=mesh,
        in_specs=(
            P("seq", "head"),
            P("head", None),
            P("seq", "head"),
            P("seq", "head"),
            P("seq", "head"),
            P("seq"),
            P(None, None, "head"),
        ),
        out_specs=(P("seq", "head"), P("seq", "head"), P("seq", "head")),
        check_vma=False,
    )
```

time: 391 us -> 61.9 us (0.16)
  waiting for transfers between devices: 306 us -> 0 us
  Pallas kernels: 0 us -> 54 us
  matrix products: 37.4 us -> 0 us
  local copies, waits for them, and re-layouts: 25.1 us -> 6.92 us
  between operations: 14.2 us -> 0.65 us
  other arithmetic: 4.27 us -> 0 us
    reduce_scatter x1 -> x0, waiting for transfers between devices: 210 us -> none  [shards(): lax.psum_scatter(jnp.einsum('ne,ehij->nhij', membership(lax.axis_size('se...]
    all_gather x2 -> x0, waiting for transfers between devices: 95.7 us -> none  [the longest x1 61.4 us: shards(): segment = lax.all_gather(device_total[None], 'seq', axis=0, tiled=True)]
    pallas_call x0 -> x1, Pallas kernels: none -> 54 us  [shards(): pl.pallas_call(functools.partial(layer, seq_size, head_size, heads), out_...]
    dot_general x25 -> x0, matrix products: 37.4 us -> none  [the longest x1 10.5 us: shards(): jnp.einsum('ne,nhij->ehij', membership(segment.shape[0]), segment, precis...]
    dot_general x1 -> x0, local copies, waits for them, and re-layouts: 8.28 us -> none  [shards(): jnp.einsum('ne,ehij->nhij', membership(lax.axis_size('seq') * 1), adjoint...]
    add x5 -> x0, local copies, waits for them, and re-layouts: 5.39 us -> none  [the longest x1 2.55 us: shards(): adjoint = adjoint + sibling(adjoint_part, bit_index)]
  transfers between devices with their start and end apart: 3 -> 0, of which waited for: 3 -> 0; matrix products, arithmetic and copies ran while one was open for 16% -> 0% of each run, Pallas kernels for 0% -> 0%
where the time goes in v1:
time: 61.9 us; the launch traced here: 61.6 us
  Pallas kernels  54 us (87%)
  local copies, waits for them, and re-layouts  6.92 us (11%)
  between operations  0.65 us (1%)
    pallas_call x1, Pallas kernels, shards(): pl.pallas_call(functools.partial(layer, seq_size, head_size, heads), out_...  54 us
    unnamed x5, local copies, waits for them, and re-layouts  5.59 us
    transpose x2, local copies, waits for them, and re-layouts, shards(): level_table[:, :levels, :].transpose(2, 1, 0)  1.33 us

profile of v1, /device:TPU:1, one launch (start us, length us, event | category | flops | bytes accessed | tf_op | source)
XLA Modules:
  0.0 61.6 jit_solution(3233334359819661628)
XLA Ops:
  0.6 0.7 %slice_bitcast_fusion = f32[4,8,128]{2,0,1:T(4,128)S(1)} fusion(f32[128,12,4]{0,2,1:T(4,128)} %param.13), kind=kLoop, calls=%fused_computation.1 | loop fusion | bytes 32768 | tf_op jit(solution)/shard_map/transpose | solution.py:374
  1.4 0.6 copy.12
  2.0 54.0 %layer.1 = (f32[512,512]{1,0:T(8,128)}, f32[512,512]{1,0:T(8,128)}, f32[512,512]{1,0:T(8,128)}) custom-call(bf16[512,512]{1,0:T(8,128)(2,1)} %y.1, bf16[512,4096]{1,0:T(8,128)(2,1)} %w.1, bf16[512,512]{1,0:T(8,128)(2,1)} %q.1, bf16[512,512]{1,0:T(8,128)(2,1)} %k.1, bf16[512,512]{1,0:T(8,128)(2,1)} %v.1, s32[1,512]{1,0:T(1,128)} %bitcast.7, f32[32,128]{1,0:T(8,128)} %bitcast.6), custom_call_target="tpu_custom_call" | custom-call | tf_op jit(solution)/shard_map/layer/pallas_call | solution.py:384
  56.0 0.0 copy-start
  56.0 2.4 %copy.16 = f32[512,512]{1,0:T(8,128)} copy(f32[512,512]{1,0:T(8,128)} %get-tuple-element.6) | data formatting | bytes 2097152
  58.3 2.3 %copy.17 = f32[512,512]{1,0:T(8,128)} copy(f32[512,512]{1,0:T(8,128)} %get-tuple-element.7) | data formatting | bytes 2097152
  60.6 0.0 copy-done
  60.6 1.0 %copy.18 = f32[512,512]{1,0:T(8,128)} copy(f32[512,512]{1,0:T(8,128)S(1)} %copy-done) | data formatting | bytes 2097152
Async XLA Ops:
  56.0 4.6 %copy-start = (f32[512,512]{1,0:T(8,128)S(1)}, f32[512,512]{1,0:T(8,128)}, u32[]{:S(2)}) copy-start(f32[512,512]{1,0:T(8,128)} %get-tuple-element.8) | copy-start | bytes 3145732

commit v2 on v1

--- a/solution.py
+++ b/solution.py
@@ -24,13 +24,13 @@
 def layer(
     seq_size, head_size, heads,
     y, w, q, k, v, rows, table,
-    qg_out, kg_out, vg_out,
-    yb, wb, qb, kb, vb, gb, qg, kg, vg,
+    qg, kg, vg,
+    yb, wb, qb, kb, vb, gb, near, levels_in, scaled_levels,
     wrow, wcol, wq, score, state, local_bucket, local_adjoint,
     total, bucket_in, bucket_sum, bucket,
-    part, part_in, part_sum, carried,
+    part, part_early, part_in, part_sum, carried,
     load_sem, own_sem, send_sem, y_sem,
-    bs1, br1, bs2, br2, as1, ar1, as2, ar2, out_sem,
+    bs1, br1, bs2, br2, as1, ar1, as2, ar2
 ):
     tokens, feats = y.shape
     width = heads * BLK
@@ -45,11 +45,12 @@
     right = lax.rem(x + 1, ring) * CORES + core
     left = lax.rem(x + ring - 1, ring) * CORES + core
     across = lax.rem(x + 2, ring) * CORES + core
+    near_chips, far_chip = (x, lax.rem(x + 1, ring), lax.rem(x + ring - 1, ring)), lax.rem(x + 2, ring)
     twin = x * CORES + 1 - core
 
     loads = [
         pltpu.make_async_copy(src, dst, load_sem.at[n])
-        for n, (src, dst) in enumerate(((k, kb), (v, vb), (q, qb), (w, wb)))
+        for n, (src, dst) in enumerate(((k, kb), (v, vb), (table, levels_in), (q, qb), (w, wb)))
     ]
     for load in loads:
         load.start()
@@ -110,15 +111,28 @@
         piece = place(across, b * BLK, BLK)
         send(piece, piece, send_sem.at[4], y_sem.at[across, b], (pos, twin))
 
-    def finish_y(b):
-        wait_y(head, b)
-        wait_y(twin, b)
-        for owner in (left, right, across):
+    def take_twin(owners, b):
+        for owner in owners:
             wait_y(owner + 1 - 2 * core, b)
 
-    def project(b):
+    def product(at, chip):
+        inner = pl.ds(pl.multiple_of(chip * CORES * feats, CORES * feats), CORES * feats)
+        return dot(yb[at, inner], wb[:, inner], NT)
+
+    def project_near(b, count):
+        for n in range(b, b + count):
+            wait_y(head, n)
+            take_twin((head, left, right), n)
+        at = pl.ds(b * BLK, count * BLK)
+        value = product(at, near_chips[0])
+        for chip in near_chips[1:]:
+            value = value + product(at, chip)
+        near[at, :] = value
+
+    def project_far(b):
+        take_twin((across,), b)
         at = pl.ds(b * BLK, BLK)
-        gb[at, :] = dot(yb[at, :], wb[...], NT).astype(BF16)
+        gb[at, :] = (near[at, :] + product(at, far_chip)).astype(BF16)
 
     def spans(bit):
         count = 2 << bit
@@ -213,13 +227,13 @@
     for bit in reversed(range(device_bits)):
         scatter_rows(bit, 0, total, bucket_in, bucket, bs1, br1, br2)
 
-    level = lax.rem(lax.broadcasted_iota(jnp.int32, table.shape, 0), levels)
-    norm = jnp.zeros(table.shape, F32)
+    loads[2].wait()
     for n in range(levels):
-        norm = jnp.where(level == n, (BLK * BLK * 2.0 ** max(n - 1, 0)) ** -0.5, norm)
-    scaled = table[...] * norm
-    hot = (lax.broadcasted_iota(jnp.int32, (table.shape[1], tokens), 0) == rows[...]).astype(BF16)
-    weight = jnp.zeros((table.shape[0], tokens), F32)
+        scale = (BLK * BLK * 2.0 ** max(n - 1, 0)) ** -0.5
+        scaled_levels[n * heads:(n + 1) * heads, :] = levels_in[n] * scale
+    scaled = scaled_levels[...]
+    hot = (lax.broadcasted_iota(jnp.int32, (scaled.shape[1], tokens), 0) == rows[...]).astype(BF16)
+    weight = jnp.zeros((scaled.shape[0], tokens), F32)
     for _ in range(3):
         piece = scaled.astype(BF16)
         scaled = scaled - piece.astype(F32)
@@ -241,7 +255,7 @@
             else:
                 local_bucket[b, m] = jnp.zeros((width, BLK), BF16)
 
-    loads[2].wait()
+    loads[3].wait()
     row_id = lax.broadcasted_iota(jnp.int32, (BLK, BLK), 0)
     col_id = lax.broadcasted_iota(jnp.int32, (BLK, BLK), 1)
     forward_near(0)
@@ -249,7 +263,7 @@
         for b in range(blocks):
             at = slice(b * BLK, (b + 1) * BLK)
             value = dot(kb[at, lanes[h]], qb[at, lanes[h]], NT)
-            value = value * jnp.where(col_id >= row_id, wrow[h * levels:h * levels + 1, at], 0.0)
+            value = value * jnp.where(col_id >= row_id, wrow[h:h + 1, at], 0.0)
             score[b, lanes[h], :] = value.astype(BF16)
     forward_near(1)
     for bit in reversed(range(device_bits)):
@@ -259,30 +273,34 @@
             at = slice(b * BLK, (b + 1) * BLK)
             turned = qb[at, lanes[h]].astype(F32).T
             for n in range(1, levels):
-                value = turned * wrow[h * levels + n:h * levels + n + 1, at]
+                value = turned * wrow[n * heads + h:n * heads + h + 1, at]
                 wq[h, (n - 1) * BLK:n * BLK, at] = value.astype(BF16)
     forward_near(2)
+    loads[4].wait()
+    pair = blocks // 2
+    project_near(0, pair)
+    for b in range(3, blocks):
+        forward_near(b)
     forward_far(0)
-    loads[3].wait()
-    finish_y(0)
-    project(0)
-    forward_near(3)
-    forward_far(1)
-    finish_y(1)
-    project(1)
-    forward_far(2)
-    finish_y(2)
-    project(2)
-    forward_far(3)
-    finish_y(3)
-    project(3)
-
-    for h in range(heads):
-        for bit in range(device_bits):
-            n = local_bits + bit
-            value = dot(wq[h, n * BLK:(n + 1) * BLK, :], gb[:, lanes[h]])
+    project_near(pair, blocks - pair)
+
+    early = slice(0, pair * BLK)
+    late = slice(pair * BLK, tokens)
+    for b in range(1, blocks):
+        forward_far(b)
+        project_far(b - 1)
+        if b == pair:
+            for h in range(heads):
+                for bit in range(device_bits):
+                    n = local_bits + bit
+                    part_early[bit, lanes[h], :] = dot(wq[h, n * BLK:(n + 1) * BLK, early], gb[early, lanes[h]])
+    project_far(blocks - 1)
+
+    for bit in reversed(range(device_bits)):
+        n = local_bits + bit
+        for h in range(heads):
+            value = part_early[bit, lanes[h], :] + dot(wq[h, n * BLK:(n + 1) * BLK, late], gb[late, lanes[h]])
             part[bit, lanes[h], :] = value.astype(BF16)
-    for bit in reversed(range(device_bits)):
         scatter_rows(bit, 1, part.at[bit], part_in, carried, as1, ar1, ar2)
 
     for h in range(heads):
@@ -301,13 +319,13 @@
         for h in range(heads):
             grad, key = gb[at, lanes[h]], kb[at, lanes[h]]
             value = dot(grad, vb[at, lanes[h]], NT)
-            value = jnp.where(row_id >= col_id, value * wcol[at, h * levels:h * levels + 1], 0.0)
+            value = jnp.where(row_id >= col_id, value * wcol[at, h:h + 1], 0.0)
             intra = value.astype(BF16)
             kg[at, lanes[h]] = dot(intra, qb[at, lanes[h]], TN)
             vg[at, lanes[h]] = dot(score[b, lanes[h], :], grad)
             value = dot(intra, key)
             for m in range(local_bits):
-                n = h * levels + 1 + m
+                n = (1 + m) * heads + h
                 value = value + wcol[at, n:n + 1] * dot(grad, local_bucket[b, m, lanes[h], :], NT)
             qg[at, lanes[h]] = value
         return 0
@@ -324,14 +342,12 @@
             grad = gb[at, lanes[h]]
             value = qg[at, lanes[h]]
             for bit in range(device_bits):
-                n = h * levels + 1 + local_bits + bit
+                n = (1 + local_bits + bit) * heads + h
                 value = value + wcol[at, n:n + 1] * dot(grad, bucket[bit, lanes[h], :], NT)
             qg[at, lanes[h]] = value
         return 0
 
     lax.fori_loop(0, blocks, outer, 0)
-    out_q = pltpu.make_async_copy(qg, qg_out, out_sem.at[0])
-    out_q.start()
 
     for bit in range(device_bits):
         wait_result(bit, 1, carried, ar2)
@@ -344,10 +360,6 @@
             adjoint = (local_adjoint[b, lanes[h], :] + sums).astype(BF16)
             kg[at, lanes[h]] += dot(vb[at, lanes[h]], adjoint, NT)
             vg[at, lanes[h]] += dot(kb[at, lanes[h]], adjoint)
-    out_k = pltpu.make_async_copy(kg, kg_out, out_sem.at[1])
-    out_v = pltpu.make_async_copy(vg, vg_out, out_sem.at[2])
-    out_k.start()
-    out_v.start()
 
     for bit in range(device_bits):
         drain(bit, 0, total, bucket_in, bs1, bs2)
@@ -357,9 +369,17 @@
     for n in range(5):
         sent = yb.at[pl.ds(0, tokens // 2 if n < 2 else tokens), pl.ds(0, feats)]
         pltpu.make_async_copy(sent, sent, send_sem.at[n]).wait()
-    out_q.wait()
-    out_k.wait()
-    out_v.wait()
+
+
+def store(qg, kg, vg, qg_out, kg_out, vg_out, sem):
+    copies = [
+        pltpu.make_async_copy(src, dst, sem.at[n])
+        for n, (src, dst) in enumerate(((qg, qg_out), (kg, kg_out), (vg, vg_out)))
+    ]
+    for copy in copies:
+        copy.start()
+    for copy in copies:
+        copy.wait()
 
 
 def shards(grad_y, w_out, queries, keys, values, level_rows, level_table):
@@ -371,7 +391,6 @@
     device_bits = seq_size.bit_length() - 1
     local_bits = blocks.bit_length() - 1
     levels = 1 + local_bits + device_bits
-    table = level_table[:, :levels, :].transpose(2, 1, 0).reshape(heads * levels, level_table.shape[0])
     hbm = pl.BlockSpec(memory_space=pl.ANY)
     vmem = pl.BlockSpec(memory_space=pltpu.VMEM)
     dma = pltpu.SemaphoreType.DMA
@@ -380,12 +399,12 @@
         pltpu.VMEM((device_bits, width // 4, BLK), BF16),
         pltpu.VMEM((device_bits, width, BLK), BF16),
     ]
-    out = jax.ShapeDtypeStruct((tokens, width), F32)
-    return pl.pallas_call(
+    table = level_table.transpose(1, 2, 0)
+    grads = pl.pallas_call(
         functools.partial(layer, seq_size, head_size, heads),
-        out_shape=(out, out, out),
-        in_specs=[hbm] * 5 + [vmem] * 2,
-        out_specs=(hbm,) * 3,
+        out_shape=(pltpu.VMEM((tokens, width), F32),) * 3,
+        in_specs=[hbm] * 5 + [vmem, hbm],
+        out_specs=(vmem,) * 3,
         scratch_shapes=[
             pltpu.VMEM((tokens, head_size * feats), BF16),
             pltpu.VMEM(w_out.shape, BF16),
@@ -394,8 +413,8 @@
             pltpu.VMEM((tokens, width), BF16),
             pltpu.VMEM((tokens, width), BF16),
             pltpu.VMEM((tokens, width), F32),
-            pltpu.VMEM((tokens, width), F32),
-            pltpu.VMEM((tokens, width), F32),
+            pltpu.VMEM(table.shape, F32),
+            pltpu.VMEM((levels * heads, table.shape[2]), F32),
             pltpu.VMEM((heads * levels, tokens), F32),
             pltpu.VMEM((tokens, BLK), F32),
             pltpu.VMEM((heads, (levels - 1) * BLK, tokens), BF16),
@@ -406,19 +425,28 @@
             pltpu.VMEM((width, BLK), BF16),
             *tree,
             pltpu.VMEM((device_bits, width, BLK), BF16),
+            pltpu.VMEM((device_bits, width, BLK), F32),
             *tree,
-            dma((4,)),
+            dma((5,)),
             dma((3,)),
             dma((5,)),
             dma((head_size, blocks)),
             *[dma((device_bits,))] * 8,
-            dma((3,)),
         ],
         compiler_params=pltpu.CompilerParams(
             collective_id=0, has_side_effects=True, vmem_limit_bytes=56 * 2**20
         ),
         name="layer",
     )(grad_y, w_out, queries, keys, values, level_rows.reshape(1, tokens), table)
+
+    return pl.pallas_call(
+        store,
+        out_shape=(jax.ShapeDtypeStruct((tokens, width), F32),) * 3,
+        in_specs=[hbm] * 3,
+        out_specs=(hbm,) * 3,
+        scratch_shapes=[dma((3,))],
+        name="store",
+    )(*[pltpu.with_memory_space_constraint(grad, pltpu.VMEM) for grad in grads])
 
 
 def solution(mesh):

time: 61.9 us -> 50.5 us (0.82)
  local copies, waits for them, and re-layouts: 6.92 us -> 0 us
  Pallas kernels: 54 us -> 49.7 us
    pallas_call x1, Pallas kernels: 54 us -> 48 us  [shards(): pl.pallas_call(functools.partial(layer, seq_size, head_size, heads), out_...]
    unnamed x5 -> x0, local copies, waits for them, and re-layouts: 5.59 us -> none
    pallas_call x0 -> x1, Pallas kernels: none -> 1.69 us  [shards(): pl.pallas_call(store, out_shape=(jax.ShapeDtypeStruct((tokens, width), F3...]
    transpose x2 -> x0, local copies, waits for them, and re-layouts: 1.33 us -> none  [shards(): level_table[:, :levels, :].transpose(2, 1, 0)]
where the time goes in v2:
time: 50.5 us; the launch traced here: 50.4 us
  Pallas kernels  49.7 us (98%)
  between operations  0.64 us (1%)
    pallas_call x1, Pallas kernels, shards(): pl.pallas_call(functools.partial(layer, seq_size, head_size, heads), out_...  48 us
    pallas_call x1, Pallas kernels, shards(): pl.pallas_call(store, out_shape=(jax.ShapeDtypeStruct((tokens, width), F3...  1.69 us

profile of v2, /device:TPU:1, one launch (start us, length us, event | category | flops | bytes accessed | tf_op | source)
XLA Modules:
  0.0 50.4 jit_solution(12341682141831840573)
XLA Ops:
  0.6 48.0 %layer.1 = (f32[512,512]{1,0:T(8,128)S(1)}, f32[512,512]{1,0:T(8,128)S(1)}, f32[512,512]{1,0:T(8,128)S(1)}) custom-call(bf16[512,512]{1,0:T(8,128)(2,1)} %y.1, bf16[512,4096]{1,0:T(8,128)(2,1)} %w.1, bf16[512,512]{1,0:T(8,128)(2,1)} %q.1, bf16[512,512]{1,0:T(8,128)(2,1)} %k.1, bf16[512,512]{1,0:T(8,128)(2,1)} %v.1, s32[1,512]{1,0:T(1,128)} %bitcast.3, ...), custom_call_target="tpu_custom_call" | custom-call | tf_op jit(solution)/shard_map/layer/pallas_call | solution.py:403
  48.7 1.7 %store.1 = (f32[512,512]{1,0:T(8,128)}, f32[512,512]{1,0:T(8,128)}, f32[512,512]{1,0:T(8,128)}) custom-call(f32[512,512]{1,0:T(8,128)S(1)} %get-tuple-element.6.qg, f32[512,512]{1,0:T(8,128)S(1)} %get-tuple-element.7.kg, f32[512,512]{1,0:T(8,128)S(1)} %get-tuple-element.8.vg), custom_call_target="tpu_custom_call" | custom-call | tf_op jit(solution)/shard_map/store/pallas_call | solution.py:442

commit v3 on v2

--- a/solution.py
+++ b/solution.py
@@ -24,11 +24,11 @@
 def layer(
     seq_size, head_size, heads,
     y, w, q, k, v, rows, table,
-    qg, kg, vg,
-    yb, wb, qb, kb, vb, gb, near, levels_in, scaled_levels,
-    wrow, wcol, wq, score, state, local_bucket, local_adjoint,
+    qg, kg, vg, kb, vb, local_adjoint, carried,
+    yb, wb, qb, gb, near, levels_in, scaled_levels,
+    wrow, wcol, wq, score, state, local_bucket,
     total, bucket_in, bucket_sum, bucket,
-    part, part_early, part_in, part_sum, carried,
+    part, part_early, part_in, part_sum,
     load_sem, own_sem, send_sem, y_sem,
     bs1, br1, bs2, br2, as1, ar1, as2, ar2
 ):
@@ -55,9 +55,6 @@
     for load in loads:
         load.start()
 
-    bucket[...] = jnp.zeros_like(bucket)
-    carried[...] = jnp.zeros_like(carried)
-
     barrier = pltpu.get_barrier_semaphore()
 
     def greet(step, _):
@@ -67,7 +64,7 @@
 
     for peer in (right, left, twin):
         pl.semaphore_signal(barrier, inc=1, device_id=(pos, peer), device_id_type=MESH)
-    lax.fori_loop(1, seq_size, greet, 0)
+    lax.fori_loop(1, seq_size, greet, 0, unroll=True)
     pl.semaphore_wait(barrier, seq_size - 1 + 3)
 
     def columns(owner):
@@ -91,6 +88,17 @@
     def wait_y(owner, b):
         here = place(owner, b * BLK, BLK)
         pltpu.make_async_copy(here, here, y_sem.at[owner, b]).wait()
+
+    for bit in range(device_bits):
+        has = lax.rem(pos // (1 << bit), 2)
+
+        @pl.when(has == 0)
+        def _():
+            bucket[bit] = jnp.zeros((width, BLK), BF16)
+
+        @pl.when(has == 1)
+        def _():
+            carried[bit] = jnp.zeros((width, BLK), BF16)
 
     half = BLK // 2
 
@@ -351,16 +359,6 @@
 
     for bit in range(device_bits):
         wait_result(bit, 1, carried, ar2)
-    for h in range(heads):
-        sums = carried[0, lanes[h], :].astype(F32)
-        for bit in range(1, device_bits):
-            sums = sums + carried[bit, lanes[h], :].astype(F32)
-        for b in range(blocks):
-            at = slice(b * BLK, (b + 1) * BLK)
-            adjoint = (local_adjoint[b, lanes[h], :] + sums).astype(BF16)
-            kg[at, lanes[h]] += dot(vb[at, lanes[h]], adjoint, NT)
-            vg[at, lanes[h]] += dot(kb[at, lanes[h]], adjoint)
-
     for bit in range(device_bits):
         drain(bit, 0, total, bucket_in, bs1, bs2)
         drain(bit, 1, part.at[bit], part_in, as1, as2)
@@ -371,13 +369,28 @@
         pltpu.make_async_copy(sent, sent, send_sem.at[n]).wait()
 
 
-def store(qg, kg, vg, qg_out, kg_out, vg_out, sem):
-    copies = [
-        pltpu.make_async_copy(src, dst, sem.at[n])
-        for n, (src, dst) in enumerate(((qg, qg_out), (kg, kg_out), (vg, vg_out)))
-    ]
-    for copy in copies:
-        copy.start()
+def finish(qg, kg, vg, kb, vb, local_adjoint, carried, qg_out, kg_out, vg_out, key_sum, value_sum, sem):
+    blocks, width, _ = local_adjoint.shape
+    copies = []
+
+    def copy_rows(src, dst, at, n):
+        copies.append(pltpu.make_async_copy(src.at[at], dst.at[at], sem.at[n]))
+        copies[-1].start()
+
+    for b in range(blocks):
+        copy_rows(qg, qg_out, pl.ds(b * BLK, BLK), b)
+    lanes = [slice(h * BLK, (h + 1) * BLK) for h in range(width // BLK)]
+    arrived = carried[0].astype(F32)
+    for bit in range(1, carried.shape[0]):
+        arrived = arrived + carried[bit].astype(F32)
+    for b in range(blocks):
+        at = slice(b * BLK, (b + 1) * BLK)
+        for lane in lanes:
+            adjoint = (local_adjoint[b, lane, :] + arrived[lane]).astype(BF16)
+            key_sum[at, lane] = kg[at, lane] + dot(vb[at, lane], adjoint, NT)
+            value_sum[at, lane] = vg[at, lane] + dot(kb[at, lane], adjoint)
+        copy_rows(key_sum, kg_out, pl.ds(b * BLK, BLK), blocks + b)
+        copy_rows(value_sum, vg_out, pl.ds(b * BLK, BLK), 2 * blocks + b)
     for copy in copies:
         copy.wait()
 
@@ -394,22 +407,21 @@
     hbm = pl.BlockSpec(memory_space=pl.ANY)
     vmem = pl.BlockSpec(memory_space=pltpu.VMEM)
     dma = pltpu.SemaphoreType.DMA
-    tree = [
-        pltpu.VMEM((device_bits, width // 2, BLK), BF16),
-        pltpu.VMEM((device_bits, width // 4, BLK), BF16),
-        pltpu.VMEM((device_bits, width, BLK), BF16),
-    ]
+    tree = pltpu.VMEM((device_bits, width // 2, BLK), BF16), pltpu.VMEM((device_bits, width // 4, BLK), BF16)
     table = level_table.transpose(1, 2, 0)
-    grads = pl.pallas_call(
+    results = pl.pallas_call(
         functools.partial(layer, seq_size, head_size, heads),
-        out_shape=(pltpu.VMEM((tokens, width), F32),) * 3,
-        in_specs=[hbm] * 5 + [vmem, hbm],
-        out_specs=(vmem,) * 3,
+        out_shape=(
+            *(pltpu.VMEM((tokens, width), F32),) * 3,
+            *(pltpu.VMEM((tokens, width), BF16),) * 2,
+            pltpu.VMEM((blocks, width, BLK), F32),
+            pltpu.VMEM((device_bits, width, BLK), BF16),
+        ),
+        in_specs=[pl.BlockSpec(memory_space=pltpu.HBM)] * 5 + [vmem, pl.BlockSpec(memory_space=pltpu.HBM)],
+        out_specs=(vmem,) * 7,
         scratch_shapes=[
             pltpu.VMEM((tokens, head_size * feats), BF16),
             pltpu.VMEM(w_out.shape, BF16),
-            pltpu.VMEM((tokens, width), BF16),
-            pltpu.VMEM((tokens, width), BF16),
             pltpu.VMEM((tokens, width), BF16),
             pltpu.VMEM((tokens, width), BF16),
             pltpu.VMEM((tokens, width), F32),
@@ -421,9 +433,9 @@
             pltpu.VMEM((blocks, width, BLK), BF16),
             pltpu.VMEM((blocks, width, BLK), F32),
             pltpu.VMEM((blocks, local_bits, width, BLK), BF16),
-            pltpu.VMEM((blocks, width, BLK), F32),
             pltpu.VMEM((width, BLK), BF16),
             *tree,
+            pltpu.VMEM((device_bits, width, BLK), BF16),
             pltpu.VMEM((device_bits, width, BLK), BF16),
             pltpu.VMEM((device_bits, width, BLK), F32),
             *tree,
@@ -434,19 +446,20 @@
             *[dma((device_bits,))] * 8,
         ],
         compiler_params=pltpu.CompilerParams(
-            collective_id=0, has_side_effects=True, vmem_limit_bytes=56 * 2**20
+            collective_id=0, has_side_effects=True, vmem_limit_bytes=54 * 2**20
         ),
         name="layer",
     )(grad_y, w_out, queries, keys, values, level_rows.reshape(1, tokens), table)
 
     return pl.pallas_call(
-        store,
+        finish,
         out_shape=(jax.ShapeDtypeStruct((tokens, width), F32),) * 3,
-        in_specs=[hbm] * 3,
+        in_specs=[vmem] * 7,
         out_specs=(hbm,) * 3,
-        scratch_shapes=[dma((3,))],
+        scratch_shapes=[pltpu.VMEM((tokens, width), F32)] * 2 + [dma((3 * blocks,))],
+        compiler_params=pltpu.CompilerParams(vmem_limit_bytes=10 * 2**20),
         name="store",
-    )(*[pltpu.with_memory_space_constraint(grad, pltpu.VMEM) for grad in grads])
+    )(*[pltpu.with_memory_space_constraint(result, pltpu.VMEM) for result in results])
 
 
 def solution(mesh):

time: 50.5 us -> 50.4 us (level)
  no operation moved by 1% of the time
where the time goes in v3:
time: 50.4 us; the launch traced here: 50.3 us
  Pallas kernels  49.7 us (99%)
  between operations  0.64 us (1%)
    pallas_call x1, Pallas kernels, shards(): pl.pallas_call(functools.partial(layer, seq_size, head_size, heads), out_...  47.9 us
    pallas_call x1, Pallas kernels, shards(): pl.pallas_call(finish, out_shape=(jax.ShapeDtypeStruct((tokens, width), F...  1.76 us

profile of v3, /device:TPU:1, one launch (start us, length us, event | category | flops | bytes accessed | tf_op | source)
XLA Modules:
  0.0 50.3 jit_solution(9831176101295171111)
XLA Ops:
  0.6 47.9 %layer.1 = (f32[512,512]{1,0:T(8,128)S(1)}, f32[512,512]{1,0:T(8,128)S(1)}, f32[512,512]{1,0:T(8,128)S(1)}, bf16[512,512]{1,0:T(8,128)(2,1)S(1)}, bf16[512,512]{...) custom-call(bf16[512,512]{1,0:T(8,128)(2,1)} %y.1, bf16[512,4096]{1,0:T(8,128)(2,1)} %w.1, ...), custom_call_target="tpu_custom_call" | custom-call | tf_op jit(solution)/shard_map/layer/pallas_call | solution.py:412
  48.6 1.8 %store.1 = (f32[512,512]{1,0:T(8,128)}, f32[512,512]{1,0:T(8,128)}, f32[512,512]{1,0:T(8,128)}) custom-call(f32[512,512]{1,0:T(8,128)S(1)} %get-tuple-element.10.qg, f32[512,512]{1,0:T(8,128)S(1)} %get-tuple-element.11.kg, f32[512,512]{1,0:T(8,128)S(1)} %get-tuple-element.12.vg, bf16[512,512]{1,0:T(8,128)(2,1)S(1)} %get-tuple-element.13.kb, ...), custom_call_target="tpu_custom_call" | custom-call | tf_op jit(solution)/shard_map/store/pallas_call | solution.py:454

commit v4 on v3

--- a/solution.py
+++ b/solution.py
@@ -274,8 +274,6 @@
             value = value * jnp.where(col_id >= row_id, wrow[h:h + 1, at], 0.0)
             score[b, lanes[h], :] = value.astype(BF16)
     forward_near(1)
-    for bit in reversed(range(device_bits)):
-        sum_rows(bit, 0, bucket_in, bucket_sum, bucket, br1, bs2, br2)
     for h in range(heads):
         for b in range(blocks):
             at = slice(b * BLK, (b + 1) * BLK)
@@ -283,19 +281,21 @@
             for n in range(1, levels):
                 value = turned * wrow[n * heads + h:n * heads + h + 1, at]
                 wq[h, (n - 1) * BLK:n * BLK, at] = value.astype(BF16)
-    forward_near(2)
+    for b in range(2, blocks):
+        forward_near(b)
+    for bit in reversed(range(device_bits)):
+        sum_rows(bit, 0, bucket_in, bucket_sum, bucket, br1, bs2, br2)
     loads[4].wait()
     pair = blocks // 2
     project_near(0, pair)
-    for b in range(3, blocks):
-        forward_near(b)
+    project_near(pair, blocks - pair)
     forward_far(0)
-    project_near(pair, blocks - pair)
 
     early = slice(0, pair * BLK)
     late = slice(pair * BLK, tokens)
     for b in range(1, blocks):
         forward_far(b)
+    for b in range(1, blocks):
         project_far(b - 1)
         if b == pair:
             for h in range(heads):

time: 50.4 us -> 49.4 us (0.980)
  Pallas kernels: 49.7 us -> 48.7 us
    pallas_call x1, Pallas kernels: 47.9 us -> 46.9 us  [shards(): pl.pallas_call(functools.partial(layer, seq_size, head_size, heads), out_...]
where the time goes in v4:
time: 49.4 us; the launch traced here: 49.3 us
  Pallas kernels  48.7 us (99%)
  between operations  0.64 us (1%)
    pallas_call x1, Pallas kernels, shards(): pl.pallas_call(functools.partial(layer, seq_size, head_size, heads), out_...  46.9 us
    pallas_call x1, Pallas kernels, shards(): pl.pallas_call(finish, out_shape=(jax.ShapeDtypeStruct((tokens, width), F...  1.76 us

profile of v4, /device:TPU:1, one launch (start us, length us, event | category | flops | bytes accessed | tf_op | source)
XLA Modules:
  0.0 49.3 jit_solution(11774064475558219958)
XLA Ops:
  0.6 46.9 %layer.1 = (f32[512,512]{1,0:T(8,128)S(1)}, f32[512,512]{1,0:T(8,128)S(1)}, f32[512,512]{1,0:T(8,128)S(1)}, bf16[512,512]{1,0:T(8,128)(2,1)S(1)}, bf16[512,512]{...) custom-call(bf16[512,512]{1,0:T(8,128)(2,1)} %y.1, bf16[512,4096]{1,0:T(8,128)(2,1)} %w.1, ...), custom_call_target="tpu_custom_call" | custom-call | tf_op jit(solution)/shard_map/layer/pallas_call | solution.py:412
  47.6 1.8 %store.1 = (f32[512,512]{1,0:T(8,128)}, f32[512,512]{1,0:T(8,128)}, f32[512,512]{1,0:T(8,128)}) custom-call(f32[512,512]{1,0:T(8,128)S(1)} %get-tuple-element.10.qg, f32[512,512]{1,0:T(8,128)S(1)} %get-tuple-element.11.kg, f32[512,512]{1,0:T(8,128)S(1)} %get-tuple-element.12.vg, bf16[512,512]{1,0:T(8,128)(2,1)S(1)} %get-tuple-element.13.kb, ...), custom_call_target="tpu_custom_call" | custom-call | tf_op jit(solution)/shard_map/store/pallas_call | solution.py:454

commit v5 on v4

--- a/solution.py
+++ b/solution.py
@@ -358,8 +358,6 @@
     lax.fori_loop(0, blocks, outer, 0)
 
     for bit in range(device_bits):
-        wait_result(bit, 1, carried, ar2)
-    for bit in range(device_bits):
         drain(bit, 0, total, bucket_in, bs1, bs2)
         drain(bit, 1, part.at[bit], part_in, as1, as2)
     for n in range(3):
@@ -367,6 +365,8 @@
     for n in range(5):
         sent = yb.at[pl.ds(0, tokens // 2 if n < 2 else tokens), pl.ds(0, feats)]
         pltpu.make_async_copy(sent, sent, send_sem.at[n]).wait()
+    for bit in range(device_bits):
+        wait_result(bit, 1, carried, ar2)
 
 
 def finish(qg, kg, vg, kb, vb, local_adjoint, carried, qg_out, kg_out, vg_out, key_sum, value_sum, sem):

time: 49.4 us -> 49.4 us (level)
  no operation moved by 1% of the time
where the time goes in v5:
time: 49.4 us; the launch traced here: 49.3 us
  Pallas kernels  48.7 us (99%)
  between operations  0.64 us (1%)
    pallas_call x1, Pallas kernels, shards(): pl.pallas_call(functools.partial(layer, seq_size, head_size, heads), out_...  46.9 us
    pallas_call x1, Pallas kernels, shards(): pl.pallas_call(finish, out_shape=(jax.ShapeDtypeStruct((tokens, width), F...  1.76 us

profile of v5, /device:TPU:1, one launch (start us, length us, event | category | flops | bytes accessed | tf_op | source)
XLA Modules:
  0.0 49.3 jit_solution(1007782076165167226)
XLA Ops:
  0.6 46.9 %layer.1 = (f32[512,512]{1,0:T(8,128)S(1)}, f32[512,512]{1,0:T(8,128)S(1)}, f32[512,512]{1,0:T(8,128)S(1)}, bf16[512,512]{1,0:T(8,128)(2,1)S(1)}, bf16[512,512]{...) custom-call(bf16[512,512]{1,0:T(8,128)(2,1)} %y.1, bf16[512,4096]{1,0:T(8,128)(2,1)} %w.1, ...), custom_call_target="tpu_custom_call" | custom-call | tf_op jit(solution)/shard_map/layer/pallas_call | solution.py:412
  47.5 1.8 %store.1 = (f32[512,512]{1,0:T(8,128)}, f32[512,512]{1,0:T(8,128)}, f32[512,512]{1,0:T(8,128)}) custom-call(f32[512,512]{1,0:T(8,128)S(1)} %get-tuple-element.10.qg, f32[512,512]{1,0:T(8,128)S(1)} %get-tuple-element.11.kg, f32[512,512]{1,0:T(8,128)S(1)} %get-tuple-element.12.vg, bf16[512,512]{1,0:T(8,128)(2,1)S(1)} %get-tuple-element.13.kb, ...), custom_call_target="tpu_custom_call" | custom-call | tf_op jit(solution)/shard_map/store/pallas_call | solution.py:454
